TPU v7x, 512 devices: a whole 4x4x16 slice. The times are simulated.
512 devices in a mesh: mp: 16 (over z), trow: 4 (over x), tcol: 8 (over y, core).
Axes of the slice: x: 4, y: 4, z: 16, core: 2. Of those that a mesh axis runs over, the one named last changes fastest.
Arguments:
- gram: float32 [16, 4096, 4096], P('mp', 'trow', 'tcol'), as said below
- rhs: float32 [256, 4096], P(('mp', 'tcol'), 'trow'), may hold values from -6 to 6
- guess: float32 [256, 4096], P(('mp', 'tcol'), 'trow'), may hold values from -6 to 6
Outputs:
- merged: float32 [256, 4096], P(('mp', 'tcol'), 'trow')
- residual: float32 [256, 4096], P(('mp', 'tcol'), 'trow')
Inputs may be any that keep to these rules, and one draw needn't show every extreme that they name: gram holds 16 symmetric positive definite matrices, one per model.
All inputs are finite; a program needn't handle non-finite values.
Results may differ from a plain program's by a relative error of at most 0.0003.
Values sent between devices are 32-bit elements; how exact they have to be, the bound alone decides.
No kernel may reach another device: no remote copies, remote signals or barrier semaphores. Data moves between devices by JAX's collectives and lax.ppermute only.
A program may use at most 64 MiB of HBM per device.

v0:
```python
import jax
import jax.numpy as jnp
from jax import lax
from jax.sharding import Mesh, PartitionSpec as P

MP = ("zh", "zl")
PLANE = ("trow", "tcol")
HIGHEST = lax.Precision.HIGHEST


def dot(lhs, rhs, lhs_dim, rhs_dim):
    return lax.dot_general(
        lhs,
        rhs,
        (((lhs_dim,), (rhs_dim,)), ((), ())),
        precision=HIGHEST,
        preferred_element_type=jnp.float32,
    )


def exchange(pieces, axes):
    return lax.all_to_all(pieces, axes, 0, 0, tiled=True)


def spread(block, axes, count):
    return exchange(jnp.broadcast_to(block[None], (count,) + block.shape), axes)


def transposed(vector, sizes):
    trow, tcol = (sizes["trow"], sizes["tcol"])
    own, wide = vector.shape
    half = wide // 2
    core = lax.axis_index("tcol") % 2
    halves = (vector[:, :half], vector[:, half:])
    got = []
    for turn in range(2):
        pairs = []
        for i in range(trow):
            for j in range(tcol):
                q, h = (j // 2, j % 2)
                pairs.append((i * tcol + j, q * tcol + 2 * i + (h ^ turn)))
        low = core == turn
        sent = jnp.where(low, halves[0], halves[1])
        got.append(lax.ppermute(sent, PLANE, pairs))
    first = core == 0
    return jnp.stack([jnp.where(first, got[0], got[1]), jnp.where(first, got[1], got[0])])


def shards(sizes, gram, rhs, guess):
    zh, zl, trow, tcol = (sizes["zh"], sizes["zl"], sizes["trow"], sizes["tcol"])
    mp = zh * zl
    tile = gram[0]
    rows, cols = tile.shape
    own = rhs.shape[0]
    thin = cols // zh
    cut = (
        tile.reshape(zl, rows // zl, zh, thin)
        .transpose(2, 0, 1, 3)
        .reshape(mp * (rows // zl), thin)
    )
    part = lax.psum_scatter(cut, MP, scatter_dimension=0, tiled=True)
    total = lax.all_gather(part, "zl", axis=0, tiled=True)
    flipped = transposed(guess, sizes)
    over_mp = spread(flipped, MP, mp)
    over_mp = over_mp.transpose(1, 0, 2, 3).reshape(2 * mp * own, cols)
    block = spread(over_mp, "trow", trow).reshape(trow * 2 * mp * own, cols)
    terms = dot(block, tile, 1, 1)
    terms = exchange(terms.reshape(tcol, mp * own, rows), "tcol").sum(0)
    terms = exchange(terms.reshape(mp, own, rows), MP).sum(0)
    first = rhs - terms
    near = spread(first, "zh", zh).reshape(zh * own, rows)
    wide = spread(near, "tcol", tcol).reshape(tcol * zh * own, rows)
    second = spread(dot(wide, total, 1, 0), "trow", trow).sum(0)
    terms = dot(second, total, 1, 1)
    pieces = jnp.concatenate([terms, second], axis=1).reshape(tcol, zh * own, rows + thin)
    pieces = exchange(pieces, "tcol")
    terms = pieces[:, :, :rows].sum(0)
    mine = lax.dynamic_slice(pieces, (2 * lax.axis_index("trow"), 0, rows), (2, zh * own, thin))
    pieces = jnp.concatenate([terms, mine[0], mine[1]], axis=1).reshape(zh, own, rows + 2 * thin)
    pieces = exchange(pieces, "zh")
    third = pieces[:, :, :rows].sum(0)
    second = pieces[:, :, rows:].reshape(zh, own, 2, thin).transpose(1, 2, 0, 3).reshape(own, rows)

    def norm(v):
        return jnp.sqrt(jnp.sum(v * v, axis=1))

    def inverse(x):
        return jnp.where(x > 0, 1.0 / jnp.where(x > 0, x, 1.0), 0.0)

    f0 = norm(first)
    e0 = first * inverse(f0)[:, None]
    s0 = jnp.sum(e0 * second, axis=1)
    rest = second - s0[:, None] * e0
    s1 = norm(rest)
    e1 = rest * inverse(s1)[:, None]
    t0 = jnp.sum(e0 * third, axis=1)
    t1 = jnp.sum(e1 * (third - t0[:, None] * e0), axis=1)
    f0, s0, s1, t0, t1 = jnp.moveaxis(spread(jnp.stack([f0, s0, s1, t0, t1]), "trow", trow), 1, 0)
    norm_first = jnp.sum(f0 * f0, 0)
    alpha = norm_first / jnp.sum(f0 * s0, 0)
    r0, r1 = (f0 - alpha * s0, -alpha * s1)
    norm_next = jnp.sum(r0 * r0 + r1 * r1, 0)
    beta = norm_next / norm_first
    d0, d1 = (r0 + beta * f0, r1)
    i0, i1 = (s0 - alpha * t0 + beta * s0, s1 - alpha * t1 + beta * s1)
    alpha_next = norm_next / jnp.sum(d0 * i0 + d1 * i1, 0)
    alpha, beta, alpha_next = (alpha[:, None], beta[:, None], alpha_next[:, None])
    residual = first - alpha * second
    direction = residual + beta * first
    image = second - alpha * third + beta * second
    merged = guess + alpha * first + alpha_next * direction
    return (merged, residual - alpha_next * image)


def solution(mesh):
    mp, trow, tcol = (mesh.shape[a] for a in ("mp", "trow", "tcol"))
    zl = 4 if mp % 4 == 0 and mp > 4 else 2
    sizes = {"zh": mp // zl, "zl": zl, "trow": trow, "tcol": tcol}
    split = Mesh(mesh.devices.reshape(tuple(sizes.values())), tuple(sizes))
    in_specs = (P(MP, "trow", "tcol"), P(MP + ("tcol",), "trow"), P(MP + ("tcol",), "trow"))
    out_specs = (P(MP + ("tcol",), "trow"), P(MP + ("tcol",), "trow"))

    def body(gram, rhs, guess):
        return shards(sizes, gram, rhs, guess)

    return jax.shard_map(body, mesh=split, in_specs=in_specs, out_specs=out_specs, check_vma=False)
```

profile of v0, /device:TPU:32, one launch (start us, length us, event | category | flops | bytes accessed | tf_op | source)
XLA Modules:
  0.0 201.9 jit_solution(11589484859543571213)
XLA Ops:
  7.2 1.9 reshape_squeeze.3
  9.2 1.6 copy.47
  10.8 0.7 copy-done.1
  11.4 0.6 collective-permute-start
  12.1 1.9 collective-permute-start.1
  14.0 1.1 collective-permute-done.1
  15.2 30.3 %all_to_all.50 = f32[16,2,2,512]{3,2,1,0:T(2,128)S(1)} all-to-all(f32[16,2,2,512]{3,2,1,0:T(2,128)S(1)} %broadcast_in_dim.21), channel_id=1, replica_groups=mesh['zh'=4,'zl'=4,'trow'=4,'tcol'=8] {'zh','zl'}, dimensions={0} | all-to-all | bytes 262144 | tf_op jit(solution)/shard_map/all_to_all | solution.py:22
  45.5 0.1 broadcast_in_dim.22
  45.7 21.8 %all_to_all.51 = f32[4,64,512]{2,1,0:T(8,128)S(1)} all-to-all(f32[4,64,512]{2,1,0:T(8,128)S(1)} %broadcast_in_dim.23), channel_id=1, replica_groups=mesh['zh'=4,'zl'=4,'trow'=4,'tcol'=8] {'trow'}, dimensions={0} | all-to-all | bytes 1048576 | tf_op jit(solution)/shard_map/all_to_all | solution.py:22
  67.5 1.9 fusion
  69.5 18.5 %all_to_all.52 = f32[8,32,1024]{2,1,0:T(8,128)S(1)} all-to-all(f32[8,32,1024]{2,1,0:T(8,128)S(1)} %fusion), channel_id=1, replica_groups=mesh['zh'=4,'zl'=4,'trow'=4,'tcol'=8] {'tcol'}, dimensions={0} | all-to-all | bytes 2097152 | tf_op jit(solution)/shard_map/all_to_all | solution.py:22
  88.0 0.1 reduce_sum.126
  88.1 0.1 reshape.100
  88.1 19.7 %all_to_all.53 = f32[16,2,1024]{2,1,0:T(2,128)S(1)} all-to-all(f32[16,2,1024]{2,1,0:T(2,128)S(1)} %reshape.100), channel_id=1, replica_groups=mesh['zh'=4,'zl'=4,'trow'=4,'tcol'=8] {'zh','zl'}, dimensions={0} | all-to-all | bytes 262144 | tf_op jit(solution)/shard_map/all_to_all | solution.py:22
  107.9 0.1 multiply_reduce_fusion.4
  108.0 16.2 %all_to_all.54 = f32[4,2,1024]{2,1,0:T(2,128)S(1)} all-to-all(f32[4,2,1024]{2,1,0:T(2,128)S(1)} %broadcast_in_dim.24), channel_id=1, replica_groups=mesh['zh'=4,'zl'=4,'trow'=4,'tcol'=8] {'zh'}, dimensions={0} | all-to-all | bytes 65536 | tf_op jit(solution)/shard_map/all_to_all | solution.py:22
  124.2 0.7 broadcast_in_dim.26
  124.9 3.4 %all-to-all-start.5 = ((f32[8,8,1024]{2,1,0:T(8,128)}), f32[8,8,1024]{2,1,0:T(8,128)S(1)}, u32[]{:S(2)}, u32[]{:S(2)}) async-start(f32[8,8,1024]{2,1,0:T(8,128)} %broadcast_in_dim.26), calls=%async_computation.5 | async-start | bytes 524288 | tf_op jit(solution)/shard_map/all_to_all | solution.py:22
  128.4 16.4 %all_gather.3 = f32[1024,128]{1,0:T(8,128)S(1)} all-gather(f32[256,128]{1,0:T(8,128)} %reduce-scatter.2.cloned.1.call-done), channel_id=1, replica_groups=mesh['zh'=4,'zl'=4,'trow'=4,'tcol'=8] {'zl'}, dimensions={0}, use_global_device_ids=true | all-gather | bytes 655360 | tf_op jit(solution)/shard_map/all_gather | solution.py:62
  144.8 0.4 fusion.2
  145.3 8.4 %all_to_all.55 = f32[4,64,128]{2,1,0:T(8,128)S(1)} all-to-all(f32[4,64,128]{2,1,0:T(8,128)S(1)} %broadcast_in_dim.27), channel_id=1, replica_groups=mesh['zh'=4,'zl'=4,'trow'=4,'tcol'=8] {'trow'}, dimensions={0} | all-to-all | bytes 262144 | tf_op jit(solution)/shard_map/all_to_all | solution.py:22
  153.6 0.7 fusion.21
  154.3 0.7 maximum_bitcast_fusion
  155.0 4.7 %all-to-all-start.7 = ((f32[8,8,1152]{2,1,0:T(8,128)}), f32[8,8,1152]{2,1,0:T(8,128)S(1)}, u32[]{:S(2)}, u32[]{:S(2)}) async-start(f32[8,8,1152]{2,1,0:T(8,128)} %maximum_bitcast_fusion), calls=%async_computation.8 | async-start | bytes 589824 | tf_op jit(solution)/shard_map/all_to_all | solution.py:22
  159.8 7.9 %all-to-all-done.7 = f32[8,8,1152]{2,1,0:T(8,128)S(1)} async-done(((f32[8,8,1152]{2,1,0:T(8,128)}), f32[8,8,1152]{2,1,0:T(8,128)S(1)}, u32[]{:S(2)}, u32[]{:S(2)}) %all-to-all-start.7) | async-done | bytes 294944 | tf_op jit(solution)/shard_map/all_to_all | solution.py:22
  167.7 0.6 pad_maximum_fusion
  168.4 3.3 %all-to-all-start.8 = ((f32[4,2,1280]{2,1,0:T(2,128)}), f32[4,2,1280]{2,1,0:T(2,128)S(1)}, u32[]{:S(2)}, u32[]{:S(2)}) async-start(f32[4,2,1280]{2,1,0:T(2,128)} %pad_maximum_fusion), calls=%async_computation.9 | async-start | bytes 81920 | tf_op jit(solution)/shard_map/all_to_all | solution.py:22
  171.7 0.1 copy.49
  171.8 12.7 %all-to-all-done.8 = f32[4,2,1280]{2,1,0:T(2,128)S(1)} async-done(((f32[4,2,1280]{2,1,0:T(2,128)}), f32[4,2,1280]{2,1,0:T(2,128)S(1)}, u32[]{:S(2)}, u32[]{:S(2)}) %all-to-all-start.8) | async-done | bytes 40992 | tf_op jit(solution)/shard_map/all_to_all | solution.py:22
  184.5 0.2 multiply_reduce_fusion.3
  184.7 0.1 copy.50
  184.8 0.2 multiply_reduce_fusion.1
  185.0 0.1 copy.51
  185.1 0.1 copy.52
  185.2 0.2 multiply_reduce_fusion
  185.4 0.1 copy.53
  185.5 0.1 stack.29
  185.6 7.6 %all_to_all.56 = f32[4,5,2]{1,2,0:T(2,128)S(1)} all-to-all(f32[4,5,2]{1,2,0:T(2,128)S(1)} %broadcast_in_dim.28), channel_id=1, replica_groups=mesh['zh'=4,'zl'=4,'trow'=4,'tcol'=8] {'trow'}, dimensions={0} | all-to-all | bytes 320 | tf_op jit(solution)/shard_map/all_to_all | solution.py:22
  193.2 0.1 fusion.20
  193.3 0.1 copy.56
  193.4 0.1 copy.55
  193.5 0.1 copy.54
  193.6 0.2 fusion.14
  193.8 0.2 fusion.13
  194.0 0.1 copy.58
  194.1 0.1 copy.57
  194.2 0.2 fusion.18
  194.4 0.7 multiply_subtract_fusion
  (35 shorter events, 0.5 us)
Async XLA Ops:
  7.2 121.2 %reduce-scatter.2.cloned.1.call-start = ((), (), s32[]{:S(2)}) async-start(), calls=%async_computation.11 | async-start | bytes 2228224 | tf_op jit(solution)/shard_map/reduce_scatter | solution.py:61
  10.7 0.7 copy-start.1
  10.7 56.8 %copy-start = (f32[1,1024,512]{2,1,0:T(8,128)S(1)}, f32[1,1024,512]{2,1,0:T(8,128)}, u32[]{:S(2)}) copy-start(f32[1,1024,512]{2,1,0:T(8,128)} %param.3) | copy-start | bytes 6291460
  11.4 2.6 %collective-permute-start = (f32[2,512]{1,0:T(2,128)S(1)}, f32[2,512]{1,0:T(2,128)S(1)}, u32[]{:S(2)}, u32[]{:S(2)}) collective-permute-start(f32[2,512]{1,0:T(2,128)S(1)} %get-tuple-element.16), channel_id=1, source_target_pairs={{0,0},{1,1},{2,8},{3,9},{4,16},{5,17},{6,24},{7,25},{8,2},{9,3},{1... | collective-permute-start | bytes 12296 | tf_op jit(solution)/shard_map/ppermute | solution.py:44
  12.1 3.1 %collective-permute-start.1 = (f32[2,512]{1,0:T(2,128)S(1)}, f32[2,512]{1,0:T(2,128)S(1)}, u32[]{:S(2)}, u32[]{:S(2)}) collective-permute-start(f32[2,512]{1,0:T(2,128)S(1)} %get-tuple-element.17), channel_id=1, source_target_pairs={{0,1},{1,0},{2,9},{3,8},{4,17},{5,16},{6,25},{7,24},{8,3},{9,2},{1... | collective-permute-start | bytes 12296 | tf_op jit(solution)/shard_map/ppermute | solution.py:44
  69.5 38.4 %copy-start.2 = (f32[2,1024]{1,0:T(2,128)S(1)}, f32[2,1024]{1,0:T(2,128)}, u32[]{:S(2)}) copy-start(f32[2,1024]{1,0:T(2,128)} %param.4) | copy-start | bytes 24580
  124.9 19.9 %all-to-all-start.5 = ((f32[8,8,1024]{2,1,0:T(8,128)}), f32[8,8,1024]{2,1,0:T(8,128)S(1)}, u32[]{:S(2)}, u32[]{:S(2)}) async-start(f32[8,8,1024]{2,1,0:T(8,128)} %broadcast_in_dim.26), calls=%async_computation.5 | async-start | bytes 524288 | tf_op jit(solution)/shard_map/all_to_all | solution.py:22
  155.0 12.6 %all-to-all-start.7 = ((f32[8,8,1152]{2,1,0:T(8,128)}), f32[8,8,1152]{2,1,0:T(8,128)S(1)}, u32[]{:S(2)}, u32[]{:S(2)}) async-start(f32[8,8,1152]{2,1,0:T(8,128)} %maximum_bitcast_fusion), calls=%async_computation.8 | async-start | bytes 589824 | tf_op jit(solution)/shard_map/all_to_all | solution.py:22
  168.4 16.1 %all-to-all-start.8 = ((f32[4,2,1280]{2,1,0:T(2,128)}), f32[4,2,1280]{2,1,0:T(2,128)S(1)}, u32[]{:S(2)}, u32[]{:S(2)}) async-start(f32[4,2,1280]{2,1,0:T(2,128)} %pad_maximum_fusion), calls=%async_computation.9 | async-start | bytes 81920 | tf_op jit(solution)/shard_map/all_to_all | solution.py:22
Sparse Core Ops, SparseCore 0:
  10.9 80.2 reduce-scatter.1
where the time goes:
time: 203 us; the launch traced here: 202 us
  blocking collectives  139 us (68%)
  waiting for transfers between devices  21.7 us (11%)
  between operations  14.3 us (7%)
  starting transfers between devices  14 us (7%)
  local copies, waits for them, and re-layouts  6.45 us (3%)
  other arithmetic  3.55 us (2%)
  matrix products  3.02 us (1%)
    all_to_all x7, blocking collectives, exchange(): return lax.all_to_all(pieces, axes, 0, 0, tiled=True)  122 us
    all_to_all x3, waiting for transfers between devices, exchange(): return lax.all_to_all(pieces, axes, 0, 0, tiled=True)  20.6 us
    all_gather x1, blocking collectives, shards(): total = lax.all_gather(part, 'zl', axis=0, tiled=True)  16.4 us
    all_to_all x3, starting transfers between devices, exchange(): return lax.all_to_all(pieces, axes, 0, 0, tiled=True)  11.4 us
  transfers between devices with their start and end apart: 6, of which 3 were waited for; matrix products, arithmetic and copies ran while one was open for 2% of the time, Pallas kernels for 0%

commit v1 on v0

--- a/solution.py
+++ b/solution.py
@@ -59,7 +59,9 @@
         .reshape(mp * (rows // zl), thin)
     )
     part = lax.psum_scatter(cut, MP, scatter_dimension=0, tiled=True)
-    total = lax.all_gather(part, "zl", axis=0, tiled=True)
+    total = jnp.concatenate(
+        lax.all_to_all(jnp.stack([part] * lax.axis_size("zl")), "zl", 0, 0), axis=0
+    )
     flipped = transposed(guess, sizes)
     over_mp = spread(flipped, MP, mp)
     over_mp = over_mp.transpose(1, 0, 2, 3).reshape(2 * mp * own, cols)

time: 203 us -> 210 us (1.034)
  the two profiles are of different devices: /device:TPU:32 before, /device:TPU:2 now
where the time goes in v1:
time: 210 us; the launch traced here: 209 us
  blocking collectives  145 us (69%)
  waiting for transfers between devices  23.9 us (11%)
  between operations  14.3 us (7%)
  starting transfers between devices  12.6 us (6%)
  local copies, waits for them, and re-layouts  6.66 us (3%)
  other arithmetic  3.55 us (2%)
  matrix products  3.02 us (1%)
    all_to_all x8, blocking collectives, exchange(): return lax.all_to_all(pieces, axes, 0, 0, tiled=True)  127 us
    all_to_all x2, waiting for transfers between devices, exchange(): return lax.all_to_all(pieces, axes, 0, 0, tiled=True)  20.5 us
    all_to_all x1, blocking collectives, shards(): lax.all_to_all(jnp.stack([part] * lax.axis_size('zl')), 'zl', 0, 0)  18.1 us
    all_to_all x2, starting transfers between devices, exchange(): return lax.all_to_all(pieces, axes, 0, 0, tiled=True)  6.69 us
    ppermute x2, starting transfers between devices, transposed(): got.append(lax.ppermute(sent, PLANE, pairs))  5.89 us
  transfers between devices with their start and end apart: 5, of which 4 were waited for; matrix products, arithmetic and copies ran while one was open for 1% of the time, Pallas kernels for 0%

profile of v1, /device:TPU:2, one launch (start us, length us, event | category | flops | bytes accessed | tf_op | source)
XLA Modules:
  0.0 208.9 jit_solution(7347073448690327831)
XLA Ops:
  7.2 1.9 reshape_squeeze.3
  9.2 1.6 copy.47
  10.8 0.7 copy-done.1
  11.4 3.4 %collective-permute-start = (f32[2,512]{1,0:T(2,128)S(1)}, f32[2,512]{1,0:T(2,128)S(1)}, u32[]{:S(2)}, u32[]{:S(2)}) collective-permute-start(f32[2,512]{1,0:T(2,128)S(1)} %get-tuple-element.16), channel_id=1, source_target_pairs={{0,0},{1,1},{2,8},{3,9},{4,16},{5,17},{6,24},{7,25},{8,2},{9,3},{1... | collective-permute-start | bytes 12296 | tf_op jit(solution)/shard_map/ppermute | solution.py:44
  14.9 2.4 %collective-permute-start.1 = (f32[2,512]{1,0:T(2,128)S(1)}, f32[2,512]{1,0:T(2,128)S(1)}, u32[]{:S(2)}, u32[]{:S(2)}) collective-permute-start(f32[2,512]{1,0:T(2,128)S(1)} %get-tuple-element.17), channel_id=1, source_target_pairs={{0,1},{1,0},{2,9},{3,8},{4,17},{5,16},{6,25},{7,24},{8,3},{9,2},{1... | collective-permute-start | bytes 12296 | tf_op jit(solution)/shard_map/ppermute | solution.py:44
  17.3 0.5 collective-permute-done
  17.8 2.9 %collective-permute-done.1 = f32[2,512]{1,0:T(2,128)S(1)} collective-permute-done((f32[2,512]{1,0:T(2,128)S(1)}, f32[2,512]{1,0:T(2,128)S(1)}, u32[]{:S(2)}, u32[]{:S(2)}) %collective-permute-start.1) | collective-permute-done | bytes 4128 | tf_op jit(solution)/shard_map/ppermute | solution.py:44
  20.8 31.4 %all_to_all.55 = f32[16,2,2,512]{3,2,1,0:T(2,128)S(1)} all-to-all(f32[16,2,2,512]{3,2,1,0:T(2,128)S(1)} %broadcast_in_dim.21), channel_id=1, replica_groups=mesh['zh'=4,'zl'=4,'trow'=4,'tcol'=8] {'zh','zl'}, dimensions={0} | all-to-all | bytes 262144 | tf_op jit(solution)/shard_map/all_to_all | solution.py:22
  52.2 0.1 broadcast_in_dim.22
  52.3 14.4 %all_to_all.56 = f32[4,64,512]{2,1,0:T(8,128)S(1)} all-to-all(f32[4,64,512]{2,1,0:T(8,128)S(1)} %broadcast_in_dim.23), channel_id=1, replica_groups=mesh['zh'=4,'zl'=4,'trow'=4,'tcol'=8] {'trow'}, dimensions={0} | all-to-all | bytes 1048576 | tf_op jit(solution)/shard_map/all_to_all | solution.py:22
  66.7 1.9 fusion
  68.7 18.5 %all_to_all.57 = f32[8,32,1024]{2,1,0:T(8,128)S(1)} all-to-all(f32[8,32,1024]{2,1,0:T(8,128)S(1)} %fusion), channel_id=1, replica_groups=mesh['zh'=4,'zl'=4,'trow'=4,'tcol'=8] {'tcol'}, dimensions={0} | all-to-all | bytes 2097152 | tf_op jit(solution)/shard_map/all_to_all | solution.py:22
  87.3 0.1 reshape.105
  87.4 20.0 %all_to_all.58 = f32[16,2,1024]{2,1,0:T(2,128)S(1)} all-to-all(f32[16,2,1024]{2,1,0:T(2,128)S(1)} %reshape.105), channel_id=1, replica_groups=mesh['zh'=4,'zl'=4,'trow'=4,'tcol'=8] {'zh','zl'}, dimensions={0} | all-to-all | bytes 262144 | tf_op jit(solution)/shard_map/all_to_all | solution.py:22
  107.4 0.1 multiply_reduce_fusion.4
  107.5 16.6 %all_to_all.59 = f32[4,2,1024]{2,1,0:T(2,128)S(1)} all-to-all(f32[4,2,1024]{2,1,0:T(2,128)S(1)} %broadcast_in_dim.24), channel_id=1, replica_groups=mesh['zh'=4,'zl'=4,'trow'=4,'tcol'=8] {'zh'}, dimensions={0} | all-to-all | bytes 65536 | tf_op jit(solution)/shard_map/all_to_all | solution.py:22
  124.2 9.9 %all_to_all.60 = f32[8,8,1024]{2,1,0:T(8,128)S(1)} all-to-all(f32[8,8,1024]{2,1,0:T(8,128)S(1)} %broadcast_in_dim.26), channel_id=1, replica_groups=mesh['zh'=4,'zl'=4,'trow'=4,'tcol'=8] {'tcol'}, dimensions={0} | all-to-all | bytes 524288 | tf_op jit(solution)/shard_map/all_to_all | solution.py:22
  134.1 0.9 stack.33
  135.1 18.1 %all_to_all.61 = f32[4,256,128]{2,1,0:T(8,128)S(1)} all-to-all(f32[4,256,128]{2,1,0:T(8,128)S(1)} %stack.33), channel_id=1, replica_groups=mesh['zh'=4,'zl'=4,'trow'=4,'tcol'=8] {'zl'}, dimensions={0} | all-to-all | bytes 1048576 | tf_op jit(solution)/shard_map/all_to_all | solution.py:63
  153.2 0.4 fusion.2
  153.6 8.4 %all_to_all.62 = f32[4,64,128]{2,1,0:T(8,128)S(1)} all-to-all(f32[4,64,128]{2,1,0:T(8,128)S(1)} %broadcast_in_dim.27), channel_id=1, replica_groups=mesh['zh'=4,'zl'=4,'trow'=4,'tcol'=8] {'trow'}, dimensions={0} | all-to-all | bytes 262144 | tf_op jit(solution)/shard_map/all_to_all | solution.py:22
  162.0 0.7 fusion.21
  162.7 0.7 maximum_bitcast_fusion
  163.4 3.4 %all-to-all-start.8 = ((f32[8,8,1152]{2,1,0:T(8,128)}), f32[8,8,1152]{2,1,0:T(8,128)S(1)}, u32[]{:S(2)}, u32[]{:S(2)}) async-start(f32[8,8,1152]{2,1,0:T(8,128)} %maximum_bitcast_fusion), calls=%async_computation.9 | async-start | bytes 589824 | tf_op jit(solution)/shard_map/all_to_all | solution.py:22
  166.9 7.8 %all-to-all-done.8 = f32[8,8,1152]{2,1,0:T(8,128)S(1)} async-done(((f32[8,8,1152]{2,1,0:T(8,128)}), f32[8,8,1152]{2,1,0:T(8,128)S(1)}, u32[]{:S(2)}, u32[]{:S(2)}) %all-to-all-start.8) | async-done | bytes 294944 | tf_op jit(solution)/shard_map/all_to_all | solution.py:22
  174.7 0.6 pad_maximum_fusion
  175.4 3.3 %all-to-all-start.9 = ((f32[4,2,1280]{2,1,0:T(2,128)}), f32[4,2,1280]{2,1,0:T(2,128)S(1)}, u32[]{:S(2)}, u32[]{:S(2)}) async-start(f32[4,2,1280]{2,1,0:T(2,128)} %pad_maximum_fusion), calls=%async_computation.10 | async-start | bytes 81920 | tf_op jit(solution)/shard_map/all_to_all | solution.py:22
  178.7 0.1 copy.49
  178.7 12.7 %all-to-all-done.9 = f32[4,2,1280]{2,1,0:T(2,128)S(1)} async-done(((f32[4,2,1280]{2,1,0:T(2,128)}), f32[4,2,1280]{2,1,0:T(2,128)S(1)}, u32[]{:S(2)}, u32[]{:S(2)}) %all-to-all-start.9) | async-done | bytes 40992 | tf_op jit(solution)/shard_map/all_to_all | solution.py:22
  191.5 0.2 multiply_reduce_fusion.3
  191.7 0.1 copy.50
  191.8 0.2 multiply_reduce_fusion.1
  192.0 0.1 copy.51
  192.1 0.1 copy.52
  192.2 0.2 multiply_reduce_fusion
  192.4 0.1 copy.53
  192.5 0.1 stack.37
  192.6 7.6 %all_to_all.63 = f32[4,5,2]{1,2,0:T(2,128)S(1)} all-to-all(f32[4,5,2]{1,2,0:T(2,128)S(1)} %broadcast_in_dim.28), channel_id=1, replica_groups=mesh['zh'=4,'zl'=4,'trow'=4,'tcol'=8] {'trow'}, dimensions={0} | all-to-all | bytes 320 | tf_op jit(solution)/shard_map/all_to_all | solution.py:22
  200.2 0.1 fusion.20
  200.3 0.1 copy.56
  200.4 0.1 copy.55
  200.5 0.1 copy.54
  200.6 0.2 fusion.14
  200.8 0.2 fusion.13
  201.0 0.1 copy.58
  201.1 0.1 copy.57
  201.2 0.2 fusion.18
  201.4 0.7 multiply_subtract_fusion
  (35 shorter events, 0.5 us)
Async XLA Ops:
  7.2 127.0 %reduce-scatter.2.cloned.1.call-start = ((), (), s32[]{:S(2)}) async-start(), calls=%async_computation.12 | async-start | bytes 2228224 | tf_op jit(solution)/shard_map/reduce_scatter | solution.py:61
  10.7 0.7 copy-start.1
  10.7 56.0 %copy-start = (f32[1,1024,512]{2,1,0:T(8,128)S(1)}, f32[1,1024,512]{2,1,0:T(8,128)}, u32[]{:S(2)}) copy-start(f32[1,1024,512]{2,1,0:T(8,128)} %param.3) | copy-start | bytes 6291460
  11.4 6.4 %collective-permute-start = (f32[2,512]{1,0:T(2,128)S(1)}, f32[2,512]{1,0:T(2,128)S(1)}, u32[]{:S(2)}, u32[]{:S(2)}) collective-permute-start(f32[2,512]{1,0:T(2,128)S(1)} %get-tuple-element.16), channel_id=1, source_target_pairs={{0,0},{1,1},{2,8},{3,9},{4,16},{5,17},{6,24},{7,25},{8,2},{9,3},{1... | collective-permute-start | bytes 12296 | tf_op jit(solution)/shard_map/ppermute | solution.py:44
  14.9 5.8 %collective-permute-start.1 = (f32[2,512]{1,0:T(2,128)S(1)}, f32[2,512]{1,0:T(2,128)S(1)}, u32[]{:S(2)}, u32[]{:S(2)}) collective-permute-start(f32[2,512]{1,0:T(2,128)S(1)} %get-tuple-element.17), channel_id=1, source_target_pairs={{0,1},{1,0},{2,9},{3,8},{4,17},{5,16},{6,25},{7,24},{8,3},{9,2},{1... | collective-permute-start | bytes 12296 | tf_op jit(solution)/shard_map/ppermute | solution.py:44
  68.7 38.7 %copy-start.2 = (f32[2,1024]{1,0:T(2,128)S(1)}, f32[2,1024]{1,0:T(2,128)}, u32[]{:S(2)}) copy-start(f32[2,1024]{1,0:T(2,128)} %param.4) | copy-start | bytes 24580
  163.4 11.2 %all-to-all-start.8 = ((f32[8,8,1152]{2,1,0:T(8,128)}), f32[8,8,1152]{2,1,0:T(8,128)S(1)}, u32[]{:S(2)}, u32[]{:S(2)}) async-start(f32[8,8,1152]{2,1,0:T(8,128)} %maximum_bitcast_fusion), calls=%async_computation.9 | async-start | bytes 589824 | tf_op jit(solution)/shard_map/all_to_all | solution.py:22
  175.4 16.1 %all-to-all-start.9 = ((f32[4,2,1280]{2,1,0:T(2,128)}), f32[4,2,1280]{2,1,0:T(2,128)S(1)}, u32[]{:S(2)}, u32[]{:S(2)}) async-start(f32[4,2,1280]{2,1,0:T(2,128)} %pad_maximum_fusion), calls=%async_computation.10 | async-start | bytes 81920 | tf_op jit(solution)/shard_map/all_to_all | solution.py:22
Sparse Core Ops, SparseCore 0:
  10.9 81.6 reduce-scatter.1
